TPU v7x, 512 devices: a whole 4x8x8 slice. The times are simulated.
512 devices in a mesh: row: 16 (over z, core), col: 32 (over x, y).
Axes of the slice: x: 4, y: 8, z: 8, core: 2. Of those that a mesh axis runs over, the one named last changes fastest.
Arguments:
- inputs: bfloat16 [1536, 6144], P('col', 'row'), may hold values from -6 to 6
- cotangent: bfloat16 [1536, 6144], P('col', 'row'), may hold values from -4 to 4
- gate_pre: bfloat16 [1536, 16384], P('row', 'col'), may hold values from -10 to 10
- up_pre: bfloat16 [1536, 16384], P('row', 'col'), may hold values from -6 to 6
- gate_weight: bfloat16 [6144, 16384], P('row', 'col'), may hold values from -0.078125 to 0.078125
- up_weight: bfloat16 [6144, 16384], P('row', 'col'), may hold values from -0.078125 to 0.078125
- down_weight: bfloat16 [16384, 6144], P('col', 'row'), may hold values from -0.046875 to 0.046875
Outputs:
- input_grad: bfloat16 [1536, 6144], P('col', 'row')
- gate_grad: bfloat16 [6144, 16384], P('row', 'col')
- up_grad: bfloat16 [6144, 16384], P('row', 'col')
- down_grad: bfloat16 [16384, 6144], P('col', 'row')
All inputs are finite; a program needn't handle non-finite values.
Results may differ from a plain program's by a relative error of at most 0.033.
Values may be sent and summed in bfloat16 or wider, within the bound.
A program may use at most 64 MiB of HBM per device.

v0:
```python
import jax
import jax.numpy as jnp
from jax import lax
from jax.sharding import PartitionSpec as P


def activate(gate_part, up_part, grad_part):
    gate_value = gate_part.astype(jnp.float32)
    up_value = up_part.astype(jnp.float32)
    sigma = jax.nn.sigmoid(gate_value)
    silu_value = gate_value * sigma
    hidden = (silu_value * up_value).astype(jnp.bfloat16)
    gate_delta = (grad_part * up_value * sigma * (1.0 + gate_value * (1.0 - sigma))).astype(
        jnp.bfloat16
    )
    up_delta = (grad_part * silu_value).astype(jnp.bfloat16)
    return (hidden, gate_delta, up_delta)


def over_tokens(left, right):
    return lax.dot_general(
        left, right, (((0,), (0,)), ((), ())), preferred_element_type=jnp.float32
    )


def over_columns(left, right):
    return lax.dot_general(
        left, right, (((1,), (1,)), ((), ())), preferred_element_type=jnp.float32
    )


def on_device(inputs, cotangent, gate_pre, up_pre, gate_weight, up_weight, down_weight):
    cotangent_all = lax.all_gather(cotangent, "col", axis=0, tiled=True)
    grad_share = lax.psum_scatter(
        over_columns(cotangent_all, down_weight).astype(jnp.bfloat16),
        "row",
        scatter_dimension=0,
        tiled=True,
    ).astype(jnp.float32)
    hidden, gate_delta, up_delta = activate(gate_pre, up_pre, grad_share)
    hidden_all, gate_all, up_all = (
        lax.all_gather(hidden, "row", axis=0, tiled=True),
        lax.all_gather(gate_delta, "row", axis=0, tiled=True),
        lax.all_gather(up_delta, "row", axis=0, tiled=True),
    )
    inputs_all = lax.all_gather(inputs, "col", axis=0, tiled=True)
    down_grad = over_tokens(hidden_all, cotangent_all).astype(jnp.bfloat16)
    gate_grad = over_tokens(inputs_all, gate_all).astype(jnp.bfloat16)
    up_grad = over_tokens(inputs_all, up_all).astype(jnp.bfloat16)
    input_grad = lax.psum_scatter(
        (over_columns(gate_all, gate_weight) + over_columns(up_all, up_weight)).astype(
            jnp.bfloat16
        ),
        "col",
        scatter_dimension=0,
        tiled=True,
    )
    return (input_grad, gate_grad, up_grad, down_grad)


def solution(mesh):
    placed = (
        P("col", "row"),
        P("col", "row"),
        P("row", "col"),
        P("row", "col"),
        P("row", "col"),
        P("row", "col"),
        P("col", "row"),
    )
    return jax.shard_map(
        on_device,
        mesh=mesh,
        in_specs=placed,
        out_specs=(P("col", "row"), P("row", "col"), P("row", "col"), P("col", "row")),
        check_vma=False,
    )
```

profile of v0, /device:TPU:1, one launch (start us, length us, event | category | flops | bytes accessed | tf_op | source)
XLA Modules:
  0.0 588.1 jit_solution(14399631066715504343)
XLA Ops:
  7.2 0.0 copy-start
  7.2 0.0 all-gather.6.cloned.1.call-start
  7.2 0.7 all-gather.6.cloned.1.call-update
  7.9 0.0 reduce-scatter.3.cloned.1.call-start
  8.0 86.2 %all-gather.6.cloned.1.call-done = bf16[1536,384]{1,0:T(8,128)(2,1)} async-done(((bf16[48,384]{1,0:T(8,128)(2,1)}), bf16[1536,384]{1,0:T(8,128)(2,1)}) %all-gather.6.cloned.1.call-update) | async-done | bytes 1179664 | tf_op jit(solution)/shard_map/all_gather | solution.py:33
  94.2 0.0 copy-done
  94.2 3.4 convolution_convert_fusion
  97.6 0.0 copy-start.5
  97.6 0.0 copy-start.6
  97.6 0.0 copy-start.3
  97.6 0.0 reduce-scatter.3.cloned.1.call-update
  97.6 0.0 all-gather.8.cloned.1.call-start
  97.7 61.2 %reduce-scatter.3.cloned.1.call-done = bf16[96,512]{1,0:T(8,128)(2,1)} async-done(((bf16[1536,512]{1,0:T(8,128)(2,1)}), bf16[96,512]{1,0:T(8,128)(2,1)}) %reduce-scatter.3.cloned.1.call-update) | async-done | bytes 98320 | tf_op jit(solution)/shard_map/reduce_scatter | solution.py:34
  158.9 0.0 copy-done.5
  158.9 0.0 copy-done.6
  158.9 1.7 fusion.7
  160.6 0.0 all-gather.8.cloned.1.call-update
  160.6 0.0 all-gather.10.cloned.1.call-start
  160.7 0.5 all-gather.10.cloned.1.call-update
  161.2 0.0 all-gather.12.cloned.1.call-start
  161.3 0.5 all-gather.12.cloned.1.call-update
  161.8 0.0 all-gather.14.cloned.1.call-start
  161.8 0.5 all-gather.14.cloned.1.call-update
  162.4 0.0 copy-start.4
  162.4 0.0 reduce-scatter.5.cloned.1.call-start
  162.4 43.1 %all-gather.8.cloned.1.call-done = bf16[1536,512]{1,0:T(8,128)(2,1)} async-done(((bf16[96,512]{1,0:T(8,128)(2,1)}), bf16[1536,512]{1,0:T(8,128)(2,1)}) %all-gather.8.cloned.1.call-update) | async-done | bytes 1572880 | tf_op jit(solution)/shard_map/all_gather | solution.py:43
  205.5 0.0 copy-done.3
  205.5 2.4 fusion.12
  208.0 41.0 %all-gather.10.cloned.1.call-done = bf16[1536,512]{1,0:T(8,128)(2,1)} async-done(((bf16[96,512]{1,0:T(8,128)(2,1)}), bf16[1536,512]{1,0:T(8,128)(2,1)}) %all-gather.10.cloned.1.call-update) | async-done | bytes 1572880 | tf_op jit(solution)/shard_map/all_gather | solution.py:44
  248.9 0.0 copy-done.4
  248.9 3.4 fusion
  252.4 0.0 reduce-scatter.5.cloned.1.call-update
  252.4 0.0 copy-start.1
  252.4 75.1 %all-gather.12.cloned.1.call-done = bf16[1536,384]{1,0:T(8,128)(2,1)} async-done(((bf16[48,384]{1,0:T(8,128)(2,1)}), bf16[1536,384]{1,0:T(8,128)(2,1)}) %all-gather.12.cloned.1.call-update) | async-done | bytes 1179664 | tf_op jit(solution)/shard_map/all_gather | solution.py:46
  327.5 2.7 fusion.1
  330.3 0.9 copy.11
  331.2 0.0 copy-done.1
  331.2 0.0 copy-start.2
  331.2 2.4 fusion.2
  333.6 0.9 copy.12
  334.5 40.9 %all-gather.14.cloned.1.call-done = bf16[1536,512]{1,0:T(8,128)(2,1)} async-done(((bf16[96,512]{1,0:T(8,128)(2,1)}), bf16[1536,512]{1,0:T(8,128)(2,1)}) %all-gather.14.cloned.1.call-update) | async-done | bytes 1572880 | tf_op jit(solution)/shard_map/all_gather | solution.py:42
  375.5 0.0 copy-done.2
  375.5 3.2 convolution_convert_fusion.1
  378.6 202.6 %reduce-scatter.5.cloned.1.call-done = bf16[48,384]{1,0:T(8,128)(2,1)} async-done(((bf16[1536,384]{1,0:T(8,128)(2,1)}), bf16[48,384]{1,0:T(8,128)(2,1)}) %reduce-scatter.5.cloned.1.call-update) | async-done | bytes 36880 | tf_op jit(solution)/shard_map/reduce_scatter | solution.py:50
Async XLA Ops:
  7.2 87.0 %copy-start = (bf16[512,384]{1,0:T(8,128)(2,1)S(1)}, bf16[512,384]{1,0:T(8,128)(2,1)}, u32[]{:S(2)}) copy-start(bf16[512,384]{1,0:T(8,128)(2,1)} %param.13) | copy-start | bytes 1179652
  7.2 87.0 %all-gather.6.cloned.1.call-start = ((), (), s32[]{:S(2)}) async-start(), calls=%async_computation.2 | async-start | bytes 1216512 | tf_op jit(solution)/shard_map/all_gather | solution.py:33
  7.9 151.0 %reduce-scatter.3.cloned.1.call-start = ((), (), s32[]{:S(2)}) async-start(), calls=%async_computation.3 | async-start | bytes 1671168 | tf_op jit(solution)/shard_map/reduce_scatter | solution.py:34
  97.6 61.3 %copy-start.5 = (bf16[96,512]{1,0:T(8,128)(2,1)S(1)}, bf16[96,512]{1,0:T(8,128)(2,1)}, u32[]{:S(2)}) copy-start(bf16[96,512]{1,0:T(8,128)(2,1)} %param.10) | copy-start | bytes 294916
  97.6 61.3 %copy-start.6 = (bf16[96,512]{1,0:T(8,128)(2,1)S(1)}, bf16[96,512]{1,0:T(8,128)(2,1)}, u32[]{:S(2)}) copy-start(bf16[96,512]{1,0:T(8,128)(2,1)} %param.9) | copy-start | bytes 294916
  97.6 107.9 %copy-start.3 = (bf16[384,512]{1,0:T(8,128)(2,1)S(1)}, bf16[384,512]{1,0:T(8,128)(2,1)}, u32[]{:S(2)}) copy-start(bf16[384,512]{1,0:T(8,128)(2,1)} %param.11) | copy-start | bytes 1179652
  97.6 107.9 %all-gather.8.cloned.1.call-start = ((), (), s32[]{:S(2)}) async-start(), calls=%async_computation.4 | async-start | bytes 1671168 | tf_op jit(solution)/shard_map/all_gather | solution.py:43
  160.6 88.3 %all-gather.10.cloned.1.call-start = ((), (), s32[]{:S(2)}) async-start(), calls=%async_computation.5 | async-start | bytes 1671168 | tf_op jit(solution)/shard_map/all_gather | solution.py:44
  161.2 166.3 %all-gather.12.cloned.1.call-start = ((), (), s32[]{:S(2)}) async-start(), calls=%async_computation.7 | async-start | bytes 1216512 | tf_op jit(solution)/shard_map/all_gather | solution.py:46
  161.8 213.7 %all-gather.14.cloned.1.call-start = ((), (), s32[]{:S(2)}) async-start(), calls=%async_computation.8 | async-start | bytes 1671168 | tf_op jit(solution)/shard_map/all_gather | solution.py:42
  162.4 86.6 %copy-start.4 = (bf16[384,512]{1,0:T(8,128)(2,1)S(1)}, bf16[384,512]{1,0:T(8,128)(2,1)}, u32[]{:S(2)}) copy-start(bf16[384,512]{1,0:T(8,128)(2,1)} %param.12) | copy-start | bytes 1179652
  162.4 418.9 %reduce-scatter.5.cloned.1.call-start = ((), (), s32[]{:S(2)}) async-start(), calls=%async_computation.6 | async-start | bytes 1216512 | tf_op jit(solution)/shard_map/reduce_scatter | solution.py:50
  252.4 78.8 %copy-start.1 = (bf16[1536,512]{1,0:T(8,128)(2,1)S(1)}, bf16[1536,512]{1,0:T(8,128)(2,1)}, u32[]{:S(2)}) copy-start(bf16[1536,512]{1,0:T(8,128)(2,1)} %all-gather.10.cloned.1.call-done) | copy-start | bytes 4718596
  331.2 44.3 %copy-start.2 = (bf16[1536,384]{1,0:T(8,128)(2,1)S(1)}, bf16[1536,384]{1,0:T(8,128)(2,1)}, u32[]{:S(2)}) copy-start(bf16[1536,384]{1,0:T(8,128)(2,1)} %all-gather.6.cloned.1.call-done) | copy-start | bytes 3538948
Sparse Core Ops, SparseCore 0:
  11.2 82.9 all-gather.5
  97.8 61.0 reduce-scatter.2
  161.8 43.6 all-gather.7
  208.3 40.5 all-gather.9
  252.4 75.0 all-gather.11
  330.3 45.1 all-gather.13
  381.1 200.1 reduce-scatter.4
where the time goes:
time: 592 us; the launch traced here: 588 us
  waiting for transfers between devices  552 us (93%)
  matrix products  17.6 us (3%)
  between operations  14.2 us (2%)
    reduce_scatter x1, waiting for transfers between devices, on_device(): lax.psum_scatter((over_columns(gate_all, gate_weight) + over_columns(up_a...  203 us
    all_gather x1, waiting for transfers between devices, on_device(): cotangent_all = lax.all_gather(cotangent, 'col', axis=0, tiled=True)  86.2 us
    all_gather x1, waiting for transfers between devices, on_device(): inputs_all = lax.all_gather(inputs, 'col', axis=0, tiled=True)  75.1 us
    reduce_scatter x1, waiting for transfers between devices, on_device(): lax.psum_scatter(over_columns(cotangent_all, down_weight).astype(jnp.bflo...  61.2 us
    all_gather x1, waiting for transfers between devices, on_device(): lax.all_gather(gate_delta, 'row', axis=0, tiled=True)  43.1 us
    all_gather x1, waiting for transfers between devices, on_device(): lax.all_gather(up_delta, 'row', axis=0, tiled=True)  41 us
    all_gather x1, waiting for transfers between devices, on_device(): lax.all_gather(hidden, 'row', axis=0, tiled=True)  40.9 us
  transfers between devices with their start and end apart: 7, of which 7 were waited for; matrix products, arithmetic and copies ran while one was open for 3% of the time, Pallas kernels for 0%

commit v1 on v0

v1 whole, which is shorter than its diff:
```python
import functools

import jax
import jax.numpy as jnp
from jax import lax
from jax.experimental import pallas as pl
from jax.experimental.pallas import tpu as pltpu
from jax.sharding import PartitionSpec as P

MESH = pl.DeviceIdType.MESH
BF16 = jnp.bfloat16
F32 = jnp.float32

N_X, N_Y, N_Z = 4, 8, 8
TOK = 48
D_OWN = 384
D_CHIP = 768
F_OWN = 512
N_SEMS = 128


def nt_dot(left, right):
    return lax.dot_general(left, right, (((1,), (1,)), ((), ())), preferred_element_type=F32)


def nn_dot(left, right):
    return lax.dot_general(left, right, (((1,), (0,)), ((), ())), preferred_element_type=F32)


def tn_dot(left, right):
    return lax.dot_general(left, right, (((0,), (0,)), ((), ())), preferred_element_type=F32)


def kernel(
    inp_in, cot_in, gate_in, up_in, wg_in, wu_in, wd_in,
    ig_out, gg_out, ug_out, dg_out,
    cot_y, inp_y, cot, inp, gate, up, wg, wu, wd,
    part, rs_send, rs_recv, hgrad, lin_g, lin_u, hidden, delta_g, delta_u,
    ig_part, xs_send, xs_recv, ig_own, ig_sib, ig_got, ys_send, ys_recv,
    dg_send, gg_send, ug_send, dg_got, gg_got, ug_got, dg_own, gg_own, ug_own,
    send_sems, recv_sems, local_sems,
):
    row = lax.axis_index("row")
    col = lax.axis_index("col")
    z, core = row // 2, row % 2
    x, y = col // N_Y, col % N_Y

    sib = (z * 2 + 1 - core, col)
    z_dev = {+1: (((z + 1) % N_Z) * 2 + core, col), -1: (((z + N_Z - 1) % N_Z) * 2 + core, col)}
    x_dev = {+1: (row, ((x + 1) % N_X) * N_Y + y), -1: (row, ((x + N_X - 1) % N_X) * N_Y + y)}
    y_dev = {+1: (row, x * N_Y + (y + 1) % N_Y), -1: (row, x * N_Y + (y + N_Y - 1) % N_Y)}

    copies = []

    def send(src, dst, device):
        k = len(copies)
        cp = pltpu.make_async_remote_copy(
            src_ref=src, dst_ref=dst, send_sem=send_sems.at[k], recv_sem=recv_sems.at[k],
            device_id=device, device_id_type=MESH,
        )
        cp.start()
        copies.append(cp)
        return cp

    local = []

    def move(src, dst):
        cp = pltpu.make_async_copy(src, dst, local_sems.at[len(local)])
        cp.start()
        local.append(cp)
        return cp

    def hops(n, long_way):
        return {long_way: n // 2, -long_way: n // 2 - 1}

    class Gather:
        def __init__(self, n, me, devs, long_way, slot, own):
            self.n, self.me, self.devs, self.slot, self.own = n, me, devs, slot, own
            self.hops = hops(n, long_way)
            self.cps = {}

        def start(self, s):
            for way in (+1, -1):
                if s <= self.hops[way]:
                    owner = (self.me - way * (s - 1) + self.n) % self.n
                    src = self.own if s == 1 else self.slot(owner)
                    self.cps[way, s] = send(src, self.slot(owner), self.devs[way])

        def wait(self, s):
            for way in (+1, -1):
                if s <= self.hops[way]:
                    self.cps[way, s].wait_recv()

    class Reduce:
        def __init__(self, n, me, devs, long_way, part, send_slot, recv_slot):
            self.n, self.me, self.devs = n, me, devs
            self.part, self.send_slot, self.recv_slot = part, send_slot, recv_slot
            self.hops = hops(n, long_way)
            self.cps = {}

        def start(self, s):
            for way in (+1, -1):
                last = self.hops[way]
                if s <= last:
                    if s > 1:
                        self.cps[way, s - 1].wait_recv()
                    dest = (self.me + way * (last - s + 1) + self.n) % self.n
                    value = self.part(dest)
                    if s > 1:
                        value = value + self.recv_slot(way, s - 1)[...].astype(F32)
                    out = self.send_slot(way, s)
                    out[...] = value.astype(BF16)
                    self.cps[way, s] = send(out, self.recv_slot(way, s), self.devs[way])

        def result(self):
            total = self.part(self.me)
            for way in (+1, -1):
                last = self.hops[way]
                self.cps[way, last].wait_recv()
                total = total + self.recv_slot(way, last)[...].astype(F32)
            return total

    barrier = pltpu.get_barrier_semaphore()
    for dev in (sib, z_dev[1], z_dev[-1], x_dev[1], x_dev[-1], y_dev[1], y_dev[-1]):
        pl.semaphore_signal(barrier, inc=1, device_id=dev, device_id_type=MESH)
    pl.semaphore_wait(barrier, 7)

    lo, hi = pl.ds(0, D_OWN), pl.ds(D_OWN, D_OWN)

    def y_slot(buf):
        return lambda yy: buf.at[yy // 4, (yy // 2) % 2, yy % 2]

    cot_ring = Gather(N_Y, y, y_dev, +1, y_slot(cot_y), cot_in)
    inp_ring = Gather(N_Y, y, y_dev, -1, y_slot(inp_y), inp_in)
    gate_ring = Gather(N_Z, z, z_dev, +1, lambda zz: gate.at[:, zz], gate_in)
    up_ring = Gather(N_Z, z, z_dev, -1, lambda zz: up.at[:, zz], up_in)

    cot_ring.start(1)
    gate_ring.start(1)
    up_ring.start(1)
    wd_cp = send(wd_in, wd.at[:, hi], sib)
    inp_ring.start(1)
    wg_cp = send(wg_in, wg.at[hi], sib)
    wu_cp = send(wu_in, wu.at[hi], sib)
    cot_self = move(cot_in, y_slot(cot_y)(y))
    inp_self = move(inp_in, y_slot(inp_y)(y))
    gate_self = move(gate_in, gate.at[:, z])
    up_self = move(up_in, up.at[:, z])
    wd_self = move(wd_in, wd.at[:, lo])
    wg_self = move(wg_in, wg.at[lo])
    wu_self = move(wu_in, wu.at[lo])

    for s in (1, 2, 3):
        cot_ring.wait(s)
        cot_ring.start(s + 1)
        inp_ring.wait(s)
        inp_ring.start(s + 1)
        if s == 2:
            gate_ring.wait(1)
            gate_ring.start(2)
            up_ring.wait(1)
            up_ring.start(2)
    cot_ring.wait(4)
    cot_self.wait()

    def halves(buf_y, buf):
        swaps = [send(buf_y.at[:, 1 - core, h], buf.at[h, pl.ds(2 * x, 2), :, hi], sib) for h in (0, 1)]
        moves = [move(buf_y.at[:, core, h], buf.at[h, pl.ds(2 * x, 2), :, lo]) for h in (0, 1)]
        for cp in moves:
            cp.wait()
        for cp in swaps:
            cp.wait_recv()

    def x_slot(buf, h, xx):
        return buf.at[h, pl.ds(2 * xx, 2)]

    def x_start(buf):
        cps = {}
        for h in (0, 1):
            for way in (+1, -1):
                hh = h if way == 1 else 1 - h
                cps[way, hh] = send(x_slot(buf, hh, x), x_slot(buf, hh, x), x_dev[way])
        return cps

    def x_forward(buf, cps):
        fwd = []
        for way, h in ((+1, 0), (-1, 1)):
            cps[way, h].wait_recv()
            owner = (x - way + N_X) % N_X
            fwd.append(send(x_slot(buf, h, owner), x_slot(buf, h, owner), x_dev[way]))
        return fwd

    def x_finish(cps, fwd):
        cps[+1, 1].wait_recv()
        cps[-1, 0].wait_recv()
        for cp in fwd:
            cp.wait_recv()

    halves(cot_y, cot)
    cot_cps = x_start(cot)
    inp_ring.wait(4)
    inp_self.wait()
    halves(inp_y, inp)
    gate_ring.wait(2)
    gate_ring.start(3)
    up_ring.wait(2)
    up_ring.start(3)
    cot_fwd = x_forward(cot, cot_cps)
    gate_ring.wait(3)
    gate_ring.start(4)
    up_ring.wait(3)
    up_ring.start(4)
    wd_self.wait()
    wd_cp.wait_recv()
    x_finish(cot_cps, cot_fwd)
    inp_cps = x_start(inp)

    for h in (0, 1):
        for n in (0, 1):
            cols = pl.ds(n * 256, 256)
            left = cot[h].reshape(8 * TOK, D_CHIP)
            part[h, :, :, cols] = nt_dot(left, wd[cols, :]).reshape(8, TOK, 256)

    red = [
        Reduce(
            N_Z, z, z_dev, +1 if h == 0 else -1,
            lambda zz, h=h: part[h, zz],
            lambda way, s, h=h: rs_send.at[h, (way + 1) // 2, s - 1],
            lambda way, s, h=h: rs_recv.at[h, (way + 1) // 2, s - 1],
        )
        for h in (0, 1)
    ]
    for h in (0, 1):
        red[h].start(1)
    for h in (0, 1):
        red[h].start(2)

    gate_ring.wait(4)
    up_ring.wait(4)
    gate_self.wait()
    up_self.wait()

    def activations(h):
        @pl.loop(0, N_Z)
        def _(zz):
            g = gate[h, zz].astype(F32)
            u = up[h, zz].astype(F32)
            s = 1.0 / (1.0 + jnp.exp(-g))
            silu = g * s
            hidden[h, zz] = (silu * u).astype(BF16)
            lin_g[h, zz] = u * s * (1.0 + g * (1.0 - s))
            lin_u[h, zz] = silu

    activations(0)
    for h in (0, 1):
        red[h].start(3)
    activations(1)
    for h in (0, 1):
        red[h].start(4)

    inp_fwd = x_forward(inp, inp_cps)

    hg_ring = [
        Gather(N_Z, z, z_dev, +1 if h == 0 else -1, lambda zz, h=h: hgrad.at[h, zz], hgrad.at[h, z])
        for h in (0, 1)
    ]
    for h in (0, 1):
        hgrad[h, z] = red[h].result().astype(BF16)
        hg_ring[h].start(1)

    hid_all = hidden.reshape(2 * N_Z * TOK, F_OWN)
    cot_all = cot.reshape(2 * N_Z * TOK, D_CHIP)
    inp_all = inp.reshape(2 * N_Z * TOK, D_CHIP)
    dgl_all = delta_g.reshape(2 * N_Z * TOK, F_OWN)
    dul_all = delta_u.reshape(2 * N_Z * TOK, F_OWN)

    @pl.loop(0, F_OWN // 128)
    def _(i):
        r = pl.ds(pl.multiple_of(i * 128, 128), 128)
        both = tn_dot(hid_all[:, r], cot_all[...])
        dg_own[r, :] = both[:, :D_OWN]
        dg_send[r, :] = both[:, D_OWN:].astype(BF16)

    dg_cp = send(dg_send, dg_got, sib)

    for s in (1, 2, 3):
        for h in (0, 1):
            hg_ring[h].wait(s)
            hg_ring[h].start(s + 1)
    x_finish(inp_cps, inp_fwd)
    wg_self.wait()
    wu_self.wait()
    wg_cp.wait_recv()
    wu_cp.wait_recv()

    def deltas(h):
        @pl.loop(0, N_Z)
        def _(zz):
            hg = hgrad[h, zz].astype(F32)
            delta_g[h, zz] = (hg * lin_g[h, zz]).astype(BF16)
            delta_u[h, zz] = (hg * lin_u[h, zz]).astype(BF16)

    def input_part(h):
        left_g = delta_g[h].reshape(N_Z * TOK, F_OWN)
        left_u = delta_u[h].reshape(N_Z * TOK, F_OWN)

        @pl.loop(0, D_CHIP // 256)
        def _(i):
            n = pl.ds(pl.multiple_of(i * 256, 256), 256)
            term = nt_dot(left_g, wg[n, :]) + nt_dot(left_u, wu[n, :])
            ig_part[h, :, :, n] = term.reshape(N_Z, TOK, 256)

    ig_red = [
        Reduce(
            N_X, x, x_dev, +1 if h == 0 else -1,
            lambda xx, h=h: ig_part[h, pl.ds(2 * xx, 2)],
            lambda way, s, h=h: xs_send.at[h, (way + 1) // 2, s - 1],
            lambda way, s, h=h: xs_recv.at[h, (way + 1) // 2, s - 1],
        )
        for h in (0, 1)
    ]
    for h in (0, 1):
        hg_ring[h].wait(4)
        deltas(h)
        input_part(h)
        ig_red[h].start(1)

    def weight_grad(delta, own, sent):
        @pl.loop(0, D_OWN // 128)
        def _(i):
            r = pl.ds(pl.multiple_of(i * 128, 128), 128)
            own[r, :] = tn_dot(inp_all[:, r], delta[...])
            r2 = pl.ds(pl.multiple_of(D_OWN + i * 128, 128), 128)
            sent[r, :] = tn_dot(inp_all[:, r2], delta[...]).astype(BF16)

    weight_grad(dgl_all, gg_own, gg_send)
    gg_cp = send(gg_send, gg_got, sib)
    for h in (0, 1):
        ig_red[h].start(2)
    weight_grad(dul_all, ug_own, ug_send)
    ug_cp = send(ug_send, ug_got, sib)

    swaps = []
    for h in (0, 1):
        total = ig_red[h].result()
        ig_own[h] = total[:, :, :D_OWN]
        ig_sib[h] = total[:, :, D_OWN:].astype(BF16)
        swaps.append(send(ig_sib.at[h], ig_got.at[h], sib))

    dg_cp.wait_recv()
    dg_out[...] = (dg_own[...] + dg_got[...].astype(F32)).astype(BF16)
    for cp in swaps:
        cp.wait_recv()

    def y_part(yy):
        h, c, k = yy % 2, (yy // 2) % 2, yy // 4
        mine = (c == core).astype(F32)
        return ig_own[h, k] * mine + ig_got[h, k].astype(F32) * (1.0 - mine)

    y_red = Reduce(
        N_Y, y, y_dev, +1, y_part,
        lambda way, s: ys_send.at[(way + 1) // 2, s - 1],
        lambda way, s: ys_recv.at[(way + 1) // 2, s - 1],
    )
    y_red.start(1)
    y_red.start(2)
    gg_cp.wait_recv()
    gg_out[...] = (gg_own[...] + gg_got[...].astype(F32)).astype(BF16)
    y_red.start(3)
    ug_cp.wait_recv()
    ug_out[...] = (ug_own[...] + ug_got[...].astype(F32)).astype(BF16)
    y_red.start(4)
    ig_out[...] = y_red.result().astype(BF16)

    for cp in copies:
        cp.wait_send()


def on_device(inputs, cotangent, gate_pre, up_pre, gate_weight, up_weight, down_weight):
    vmem = pl.BlockSpec(memory_space=pltpu.VMEM)
    shape = jax.ShapeDtypeStruct
    scratch = [
        pltpu.VMEM((2, 2, 2, TOK, D_OWN), BF16),
        pltpu.VMEM((2, 2, 2, TOK, D_OWN), BF16),
        pltpu.VMEM((2, N_Z, TOK, D_CHIP), BF16),
        pltpu.VMEM((2, N_Z, TOK, D_CHIP), BF16),
        pltpu.VMEM((2, N_Z, TOK, F_OWN), BF16),
        pltpu.VMEM((2, N_Z, TOK, F_OWN), BF16),
        pltpu.VMEM((D_CHIP, F_OWN), BF16),
        pltpu.VMEM((D_CHIP, F_OWN), BF16),
        pltpu.VMEM((F_OWN, D_CHIP), BF16),
        pltpu.VMEM((2, N_Z, TOK, F_OWN), F32),
        pltpu.VMEM((2, 2, 4, TOK, F_OWN), BF16),
        pltpu.VMEM((2, 2, 4, TOK, F_OWN), BF16),
        pltpu.VMEM((2, N_Z, TOK, F_OWN), BF16),
        pltpu.VMEM((2, N_Z, TOK, F_OWN), F32),
        pltpu.VMEM((2, N_Z, TOK, F_OWN), F32),
        pltpu.VMEM((2, N_Z, TOK, F_OWN), BF16),
        pltpu.VMEM((2, N_Z, TOK, F_OWN), BF16),
        pltpu.VMEM((2, N_Z, TOK, F_OWN), BF16),
        pltpu.VMEM((2, N_Z, TOK, D_CHIP), F32),
        pltpu.VMEM((2, 2, 2, 2, TOK, D_CHIP), BF16),
        pltpu.VMEM((2, 2, 2, 2, TOK, D_CHIP), BF16),
        pltpu.VMEM((2, 2, TOK, D_OWN), F32),
        pltpu.VMEM((2, 2, TOK, D_OWN), BF16),
        pltpu.VMEM((2, 2, TOK, D_OWN), BF16),
        pltpu.VMEM((2, 4, TOK, D_OWN), BF16),
        pltpu.VMEM((2, 4, TOK, D_OWN), BF16),
        pltpu.VMEM((F_OWN, D_OWN), BF16),
        pltpu.VMEM((D_OWN, F_OWN), BF16),
        pltpu.VMEM((D_OWN, F_OWN), BF16),
        pltpu.VMEM((F_OWN, D_OWN), BF16),
        pltpu.VMEM((D_OWN, F_OWN), BF16),
        pltpu.VMEM((D_OWN, F_OWN), BF16),
        pltpu.VMEM((F_OWN, D_OWN), F32),
        pltpu.VMEM((D_OWN, F_OWN), F32),
        pltpu.VMEM((D_OWN, F_OWN), F32),
        pltpu.SemaphoreType.DMA((N_SEMS,)),
        pltpu.SemaphoreType.DMA((N_SEMS,)),
        pltpu.SemaphoreType.DMA((16,)),
    ]
    return pl.pallas_call(
        kernel,
        out_shape=(
            shape((TOK, D_OWN), BF16),
            shape((D_OWN, F_OWN), BF16),
            shape((D_OWN, F_OWN), BF16),
            shape((F_OWN, D_OWN), BF16),
        ),
        in_specs=[vmem] * 7,
        out_specs=(vmem,) * 4,
        scratch_shapes=scratch,
        compiler_params=pltpu.CompilerParams(
            collective_id=0, has_side_effects=True, vmem_limit_bytes=56 * 1024 * 1024
        ),
        cost_estimate=pl.CostEstimate(
            flops=3_700_000_000, bytes_accessed=3_000_000, transcendentals=400_000
        ),
    )(
        inputs,
        cotangent,
        gate_pre.reshape(2, TOK, F_OWN),
        up_pre.reshape(2, TOK, F_OWN),
        gate_weight,
        up_weight,
        down_weight,
    )


def solution(mesh):
    placed = (
        P("col", "row"),
        P("col", "row"),
        P("row", "col"),
        P("row", "col"),
        P("row", "col"),
        P("row", "col"),
        P("col", "row"),
    )
    return jax.shard_map(
        on_device,
        mesh=mesh,
        in_specs=placed,
        out_specs=(P("col", "row"), P("row", "col"), P("row", "col"), P("col", "row")),
        check_vma=False,
    )
```

time: 592 us -> 105 us (0.18)
  waiting for transfers between devices: 552 us -> 0 us
  Pallas kernels: 0 us -> 98.2 us
  matrix products: 17.6 us -> 0 us
  between operations: 14.2 us -> 0.64 us
    all_gather x5 -> x0, waiting for transfers between devices: 286 us -> none  [the longest x1 86.2 us: on_device(): cotangent_all = lax.all_gather(cotangent, 'col', axis=0, tiled=True)]
    reduce_scatter x2 -> x0, waiting for transfers between devices: 264 us -> none  [the longest x1 203 us: on_device(): lax.psum_scatter((over_columns(gate_all, gate_weight) + over_columns(up_a...]
    pallas_call x0 -> x1, Pallas kernels: none -> 98.2 us  [on_device(): pl.pallas_call(kernel, out_shape=(shape((TOK, D_OWN), BF16), shape((D_OWN...]
    dot_general x6 -> x0, matrix products: 17.6 us -> none  [the longest x3 9.3 us: over_columns(): lax.dot_general(left, right, (((1,), (1,)), ((), ())), preferred_element_...]
  transfers between devices with their start and end apart: 7 -> 0, of which waited for: 7 -> 0; matrix products, arithmetic and copies ran while one was open for 3% -> 0% of each run, Pallas kernels for 0% -> 0%
where the time goes in v1:
time: 105 us; the launch traced here: 104 us
  Pallas kernels  98.2 us (94%)
  local copies, waits for them, and re-layouts  5.09 us (5%)
    pallas_call x1, Pallas kernels, on_device(): pl.pallas_call(kernel, out_shape=(shape((TOK, D_OWN), BF16), shape((D_OWN...  98.2 us
    unnamed x8, local copies, waits for them, and re-layouts  5.09 us

profile of v1, /device:TPU:1, one launch (start us, length us, event | category | flops | bytes accessed | tf_op | source)
XLA Modules:
  0.0 103.9 jit_solution(17225384030207443350)
XLA Ops:
  0.6 98.2 %shard_map.102 = (bf16[48,384]{1,0:T(8,128)(2,1)}, bf16[384,512]{1,0:T(8,128)(2,1)}, bf16[384,512]{1,0:T(8,128)(2,1)}, bf16[512,384]{1,0:T(8,128)(2,1)}) custom-call(bf16[48,384]{1,0:T(8,128)(2,1)} %inp_in.1, bf16[48,384]{1,0:T(8,128)(2,1)} %cot_in.1, bf16[2,48,512]{2,1,0:T(8,128)(2,1)} %bitcast.2, bf16[2,48,512]{2,1,0:T(8,128)(2,1)} %bitcast.3, ...), custom_call_target="tpu_custom_call" | custom-call | flops 3700000000 | bytes 3000000 | tf_op jit(solution)/shard_map/pallas_call | solution.py:422
  98.8 1.4 %copy.15 = bf16[48,384]{1,0:T(8,128)(2,1)} copy(bf16[48,384]{1,0:T(8,128)(2,1)} %get-tuple-element.8) | data formatting | bytes 73728
  100.2 0.0 copy-start.1
  100.2 1.8 %copy.16 = bf16[384,512]{1,0:T(8,128)(2,1)} copy(bf16[384,512]{1,0:T(8,128)(2,1)} %get-tuple-element.9) | data formatting | bytes 786432
  102.1 0.0 copy-done.1
  102.1 0.0 copy-start
  102.1 0.7 copy.17
  102.8 0.4 copy-done
  103.2 0.7 copy.18
Async XLA Ops:
  100.2 1.8 %copy-start.1 = (bf16[384,512]{1,0:T(8,128)(2,1)S(1)}, bf16[384,512]{1,0:T(8,128)(2,1)}, u32[]{:S(2)}) copy-start(bf16[384,512]{1,0:T(8,128)(2,1)} %get-tuple-element.10) | copy-start | bytes 1179652
  102.1 1.1 %copy-start = (bf16[512,384]{1,0:T(8,128)(2,1)S(1)}, bf16[512,384]{1,0:T(8,128)(2,1)}, u32[]{:S(2)}) copy-start(bf16[512,384]{1,0:T(8,128)(2,1)} %get-tuple-element.11) | copy-start | bytes 1179652

commit v2 on v0

v2 whole, which is shorter than its diff:
```python
import jax
import jax.numpy as jnp
from jax import lax
from jax.experimental import pallas as pl
from jax.experimental.pallas import tpu as pltpu
from jax.sharding import PartitionSpec as P

MESH = pl.DeviceIdType.MESH
BF16 = jnp.bfloat16
F32 = jnp.float32

N_X, N_Y, N_Z = 4, 8, 8
TOK = 48
D_OWN = 384
D_CHIP = 768
F_OWN = 512
CHUNK = 192
F_PART = 128
N_SEMS = 200


def nt_dot(left, right):
    return lax.dot_general(left, right, (((1,), (1,)), ((), ())), preferred_element_type=F32)


def tn_dot(left, right):
    return lax.dot_general(left, right, (((0,), (0,)), ((), ())), preferred_element_type=F32)


def kernel(
    inp_in, cot_in, gate_in, up_in, wg_in, wu_in, wd_in,
    ig_out, gg_out, ug_out, dg_out,
    cot, inp, gate, up, wg, wu, wd,
    part, part16, near_got, far_got, half_got, pair_got, pair_send, hgrad,
    lin_g, lin_u, hidden, delta_g, delta_u,
    ig_mine, xs_send, xs_got, ys_send, ys_got,
    dg_send, gg_send, ug_send, dg_got, gg_got, ug_got, dg_own, gg_own, ug_own,
    ig_sum, gg_sum, ug_sum, dg_sum,
    send_sems, recv_sems, local_sems, cot_sems, inp_sems, ys_sems,
):
    row = lax.axis_index("row")
    col = lax.axis_index("col")
    z, core = row // 2, row % 2
    x, y = col // N_Y, col % N_Y

    def at_z(dz):
        return (((z + dz + N_Z) % N_Z) * 2 + core, col)

    def at_x(dx):
        return (row, ((x + dx + N_X) % N_X) * N_Y + y)

    def at_y(dy, on_core):
        return (z * 2 + on_core, x * N_Y + (y + dy) % N_Y)

    sib = at_y(0, 1 - core)

    copies = []
    local = []

    def send(src, dst, device):
        k = len(copies)
        cp = pltpu.make_async_remote_copy(
            src_ref=src, dst_ref=dst, send_sem=send_sems.at[k], recv_sem=recv_sems.at[k],
            device_id=device, device_id_type=MESH,
        )
        cp.start()
        copies.append(cp)
        return cp

    def move(src, dst):
        cp = pltpu.make_async_copy(src, dst, local_sems.at[len(local)])
        cp.start()
        local.append(cp)
        return cp

    barrier = pltpu.get_barrier_semaphore()
    others = [sib] + [at_y(dy, c) for dy in range(1, N_Y) for c in (0, 1)]
    others += [at_x(dx) for dx in (1, 2, 3)] + [at_z(dz) for dz in (1, 2, 6, 7)]
    for dev in others:
        pl.semaphore_signal(barrier, inc=1, device_id=dev, device_id_type=MESH)
    pl.semaphore_wait(barrier, len(others))

    lo, hi = pl.ds(0, D_OWN), pl.ds(D_OWN, D_OWN)

    def chunk_of(xx):
        dx = (xx - x + N_X) % N_X
        return dx + (dx // 2) * (5 - 2 * dx)

    c_y, k_y, h_y = (y // 2) % 2, y // 4, y % 2
    side = (core + c_y) % 2
    y_sem = (k_y * 2 + h_y) * 2 + side
    late_sends = []

    def over_y(src, buf, sems):
        dst = buf.at[0, k_y, h_y, :, pl.ds(pl.multiple_of(side * D_OWN, 128), D_OWN)]

        def copy(k, device):
            return pltpu.make_async_remote_copy(
                src_ref=src, dst_ref=dst, send_sem=send_sems.at[k], recv_sem=sems.at[y_sem],
                device_id=device, device_id_type=MESH,
            )

        for dy in (4, 3, 5, 2, 6, 1, 7):
            cp = copy(len(copies), at_y(dy, c_y))
            cp.start()
            copies.append(cp)
        k = N_SEMS - 1 - len(late_sends)
        late_sends.append((lambda: copy(k, sib), side == 1))

        @pl.when(side == 0)
        def _():
            pltpu.make_async_copy(src, dst, sems.at[y_sem]).start()

        @pl.when(side == 1)
        def _():
            copy(k, sib).start()

    def over_y_wait(buf, sems):
        for k in (0, 1):
            for h in (0, 1):
                for s, cols in ((0, lo), (1, hi)):
                    dst = buf.at[0, k, h, :, cols]
                    pltpu.make_async_copy(dst, dst, sems.at[(k * 2 + h) * 2 + s]).wait()

    def over_x(buf):
        return [send(buf.at[0], buf.at[r], at_x(dx)) for dx, r in ((2, 3), (1, 2), (3, 1))]

    class Ring:
        def __init__(self, buf, own, long_way):
            self.buf, self.own = buf, own
            self.hops = {long_way: N_Z // 2, -long_way: N_Z // 2 - 1}
            self.cps = {}

        def slot(self, zz):
            return self.buf.at[chunk_of(zz // 2), zz % 2]

        def start(self, s):
            for way in (+1, -1):
                if s <= self.hops[way]:
                    owner = (z - way * (s - 1) + N_Z) % N_Z
                    src = self.own if s == 1 else self.slot(owner)
                    self.cps[way, s] = send(src, self.slot(owner), at_z(way))

        def wait(self, s):
            for way in (+1, -1):
                if s <= self.hops[way]:
                    self.cps[way, s].wait_recv()

    def piece(buf, r, dz, rows=pl.ds(0, 2 * TOK)):
        o = (z + dz + N_Z) % N_Z
        return buf.at[r, o // 4, rows, pl.ds(pl.multiple_of((o % 4) * F_PART, F_PART), F_PART)]

    halves = {+1: pl.ds(0, TOK), -1: pl.ds(TOK, TOK)}

    class SumOverZ:
        def __init__(self, r):
            self.r = r
            self.cps = {}

        def first(self):
            r = self.r
            for i, way in enumerate((+1, -1)):
                self.cps["far", way] = send(piece(part16, r, 3 * way), far_got.at[r, i], at_z(way))
                self.cps["half", way] = send(
                    piece(part16, r, 4, halves[way]), half_got.at[r, i], at_z(2 * way)
                )
            for i, way in enumerate((+1, -1)):
                self.cps["near", way] = send(piece(part16, r, way), near_got.at[r, i], at_z(way))

        def second(self):
            r = self.r
            for i, way in enumerate((+1, -1)):
                self.cps["far", way].wait_recv()
                self.cps["half", way].wait_recv()
                total = piece(part, r, 2 * way)[...] + far_got[r, i].astype(F32)
                extra = half_got[r, i].astype(F32)
                rest = jnp.zeros_like(extra)
                rows = (extra, rest) if way == 1 else (rest, extra)
                pair_send[r, i] = (total + jnp.concatenate(rows, axis=0)).astype(BF16)
                self.cps["pair", way] = send(pair_send.at[r, i], pair_got.at[r, i], at_z(2 * way))

        def third(self):
            r = self.r
            total = piece(part, r, 0)[...]
            for i, way in enumerate((+1, -1)):
                self.cps["near", way].wait_recv()
                total = total + near_got[r, i].astype(F32)
            for i, way in enumerate((+1, -1)):
                self.cps["pair", way].wait_recv()
                total = total + pair_got[r, i].astype(F32)
            own = piece(hgrad, r, 0)
            own[...] = total.astype(BF16)
            for way in (+1, -1):
                self.cps["all2", way] = send(own, own, at_z(2 * way))
            for way in (+1, -1):
                self.cps["all1", way] = send(own, own, at_z(way))

        def fourth(self):
            r = self.r
            for way in (+1, -1):
                self.cps["all2", way].wait_recv()
                got = piece(hgrad, r, -2 * way)
                self.cps["all3", way] = send(got, got, at_z(way))
                got = piece(hgrad, r, -2 * way, halves[way])
                self.cps["all4", way] = send(got, got, at_z(2 * way))

        def last(self):
            for way in (+1, -1):
                for name in ("all1", "all3", "all4"):
                    self.cps[name, way].wait_recv()

    def partial_sums(r):
        left = cot[r].reshape(CHUNK, D_CHIP)
        for n in (0, 1):
            cols = pl.ds(n * 256, 256)
            value = nt_dot(left, wd[cols, :]).reshape(2, 2 * TOK, 256)
            part[r, :, :, cols] = value
            part16[r, :, :, cols] = value.astype(BF16)

    def activations(r):
        @pl.loop(0, 4)
        def _(i):
            rows = pl.ds(pl.multiple_of((i % 2) * TOK, TOK), TOK)
            g = gate[r, i // 2, rows].astype(F32)
            u = up[r, i // 2, rows].astype(F32)
            s = 1.0 / (1.0 + jnp.exp(-g))
            silu = g * s
            hidden[r, i // 2, rows] = (silu * u).astype(BF16)
            lin_g[r, i // 2, rows] = u * s * (1.0 + g * (1.0 - s))
            lin_u[r, i // 2, rows] = silu

    def deltas(r):
        @pl.loop(0, 4)
        def _(i):
            rows = pl.ds(pl.multiple_of((i % 2) * TOK, TOK), TOK)
            hg = hgrad[r, i // 2, rows].astype(F32)
            delta_g[r, i // 2, rows] = (hg * lin_g[r, i // 2, rows]).astype(BF16)
            delta_u[r, i // 2, rows] = (hg * lin_u[r, i // 2, rows]).astype(BF16)

    def input_part(r):
        left_g = delta_g[r].reshape(CHUNK, F_OWN)
        left_u = delta_u[r].reshape(CHUNK, F_OWN)
        for i in range(D_CHIP // 256):
            n = pl.ds(i * 256, 256)
            term = nt_dot(left_g, wg[n, :]) + nt_dot(left_u, wu[n, :])
            term = term.reshape(2, 2 * TOK, 256)
            if r == 0:
                ig_mine[:, :, n] = term
            else:
                xs_send[r - 1, :, :, n] = term.astype(BF16)

    xs_cps = {}

    def send_x(r):
        dx = {1: 1, 2: 3, 3: 2}[r]
        for k in (0, 1):
            xs_cps[r, k] = send(xs_send.at[r - 1, k], xs_got.at[r - 1, k], at_x(dx))

    late_ys = []

    def send_y(k):
        total = ig_mine[k]
        for r in (1, 2, 3):
            xs_cps[r, k].wait_recv()
            total = total + xs_got[r - 1, k].astype(F32)
        ys_send[k] = total.astype(BF16)
        for h in (0, 1):
            yy = 4 * k + 2 * core + h
            rows = pl.ds(h * TOK, TOK)

            def copy(q, cols, on_core, rows=rows, yy=yy):
                return pltpu.make_async_remote_copy(
                    src_ref=ys_send.at[k, rows, cols], dst_ref=ys_got.at[y],
                    send_sem=send_sems.at[q], recv_sem=ys_sems.at[y],
                    device_id=(z * 2 + on_core, x * N_Y + yy), device_id_type=MESH,
                )

            cp = copy(len(copies), hi, 1 - core)
            cp.start()
            copies.append(cp)
            q = N_SEMS - 1 - len(late_sends)
            late_sends.append((lambda q=q, copy=copy: copy(q, lo, core), yy != y))

            @pl.when(yy != y)
            def _(q=q, copy=copy):
                copy(q, lo, core).start()

            @pl.when(yy == y)
            def _(k=k, rows=rows):
                pltpu.make_async_copy(ys_send.at[k, rows, lo], ys_got.at[y], ys_sems.at[y]).start()

    def flat(buf, first, count, width):
        return buf.at[pl.ds(first, count)].reshape(count * CHUNK, width)

    def down_grad():
        left = flat(hidden, 0, 4, F_OWN)
        right = flat(cot, 0, 4, D_CHIP)

        @pl.loop(0, F_OWN // 128)
        def _(i):
            rows = pl.ds(pl.multiple_of(i * 128, 128), 128)
            both = tn_dot(left[:, rows], right[...])
            dg_own[rows, :] = both[:, :D_OWN]
            dg_send[rows, :] = both[:, D_OWN:].astype(BF16)

        return send(dg_send, dg_got, sib)

    def weight_grad(delta, own, first, count, sent=None):
        left = flat(inp, first, count, D_CHIP)
        right = flat(delta, first, count, F_OWN)

        @pl.loop(0, D_CHIP // 128)
        def _(i):
            rows = pl.ds(pl.multiple_of(i * 128, 128), 128)
            value = tn_dot(left[:, rows], right[...])
            if first > 0:
                value = value + own[rows, :]
            own[rows, :] = value

        if sent is not None:
            sent[...] = own[hi, :].astype(BF16)

    def finish(own, got, cp, total, out):
        cp.wait_recv()
        total[...] = (own[pl.ds(0, total.shape[0]), :] + got[...].astype(F32)).astype(BF16)
        return move(total, out)

    over_y(cot_in, cot, cot_sems)
    gate_ring = Ring(gate, gate_in, +1)
    up_ring = Ring(up, up_in, -1)
    gate_ring.start(1)
    up_ring.start(1)
    wd_self = move(wd_in, wd.at[:, lo])
    wd_cp = send(wd_in, wd.at[:, hi], sib)
    gate_self = move(gate_in, gate_ring.slot(z))
    up_self = move(up_in, up_ring.slot(z))

    over_y_wait(cot, cot_sems)
    cot_cps = over_x(cot)
    over_y(inp_in, inp, inp_sems)
    wd_self.wait()
    wd_cp.wait_recv()
    partial_sums(0)
    sums = [SumOverZ(r) for r in range(4)]
    sums[0].first()
    gate_ring.wait(1)
    gate_ring.start(2)
    up_ring.wait(1)
    up_ring.start(2)
    wg_self = move(wg_in, wg.at[lo])
    wu_self = move(wu_in, wu.at[lo])
    wg_cp = send(wg_in, wg.at[hi], sib)
    wu_cp = send(wu_in, wu.at[hi], sib)
    gate_self.wait()
    up_self.wait()

    sums[0].second()
    gate_ring.wait(2)
    gate_ring.start(3)
    up_ring.wait(2)
    up_ring.start(3)
    cot_cps[1].wait_recv()
    partial_sums(2)
    sums[2].first()
    cot_cps[2].wait_recv()
    partial_sums(1)
    sums[1].first()
    sums[0].third()
    cot_cps[0].wait_recv()
    partial_sums(3)
    sums[3].first()
    over_y_wait(inp, inp_sems)
    inp_cps = over_x(inp)
    gate_ring.wait(3)
    gate_ring.start(4)
    up_ring.wait(3)
    up_ring.start(4)
    sums[2].second()
    sums[1].second()
    sums[0].fourth()
    sums[3].second()
    sums[2].third()
    sums[1].third()
    gate_ring.wait(4)
    up_ring.wait(4)
    activations(0)
    sums[3].third()
    activations(2)
    activations(1)
    sums[2].fourth()
    sums[1].fourth()
    activations(3)
    wg_self.wait()
    wu_self.wait()
    wg_cp.wait_recv()
    wu_cp.wait_recv()
    sums[0].last()
    deltas(0)
    input_part(0)
    sums[3].fourth()
    sums[2].last()
    deltas(2)
    input_part(2)
    send_x(2)
    sums[1].last()
    deltas(1)
    input_part(1)
    send_x(1)
    dg_cp = down_grad()
    sums[3].last()
    deltas(3)
    input_part(3)
    send_x(3)
    for cp in inp_cps:
        cp.wait_recv()
    weight_grad(delta_g, gg_own, 0, 3)
    weight_grad(delta_g, gg_own, 3, 1, gg_send)
    gg_cp = send(gg_send, gg_got, sib)
    outs = [finish(dg_own, dg_got, dg_cp, dg_sum, dg_out)]
    send_y(0)
    send_y(1)
    weight_grad(delta_u, ug_own, 0, 3)
    weight_grad(delta_u, ug_own, 3, 1, ug_send)
    ug_cp = send(ug_send, ug_got, sib)
    outs.append(finish(gg_own, gg_got, gg_cp, gg_sum, gg_out))
    outs.append(finish(ug_own, ug_got, ug_cp, ug_sum, ug_out))

    total = jnp.zeros((TOK, D_OWN), F32)
    for yy in range(N_Y):
        dst = ys_got.at[yy]
        pltpu.make_async_copy(dst, dst, ys_sems.at[yy]).wait()
        total = total + ys_got[yy].astype(F32)
    ig_sum[...] = total.astype(BF16)
    outs.append(move(ig_sum, ig_out))

    for cp in copies:
        cp.wait_send()
    for make, remote in late_sends:
        @pl.when(remote)
        def _(make=make):
            make().wait_send()
    for cp in outs:
        cp.wait()


def copy_kernel(a, b, c, d, a_out, b_out, c_out, d_out, a_buf, b_buf, c_buf, d_buf, sems):
    sets = ((a, a_buf, a_out), (b, b_buf, b_out), (c, c_buf, c_out), (d, d_buf, d_out))
    reads = [pltpu.make_async_copy(src, buf, sems.at[i]) for i, (src, buf, _) in enumerate(sets)]
    writes = [pltpu.make_async_copy(buf, dst, sems.at[4 + i]) for i, (_, buf, dst) in enumerate(sets)]
    for cp in reads:
        cp.start()
    for before, cp in zip(reads, writes):
        before.wait()
        cp.start()
    for cp in writes:
        cp.wait()


def on_device(inputs, cotangent, gate_pre, up_pre, gate_weight, up_weight, down_weight):
    vmem = pl.BlockSpec(memory_space=pltpu.VMEM)
    hbm = pl.BlockSpec(memory_space=pl.ANY)
    shape = jax.ShapeDtypeStruct
    outs = (
        shape((TOK, D_OWN), BF16),
        shape((D_OWN, F_OWN), BF16),
        shape((D_OWN, F_OWN), BF16),
        shape((F_OWN, D_OWN), BF16),
    )
    by_token = lambda width, kind: pltpu.VMEM((4, 2, 2 * TOK, width), kind)
    z_piece = pltpu.VMEM((4, 2, 2 * TOK, F_PART), BF16)
    scratch = [
        pltpu.VMEM((4, 2, 2, TOK, D_CHIP), BF16),
        pltpu.VMEM((4, 2, 2, TOK, D_CHIP), BF16),
        by_token(F_OWN, BF16),
        by_token(F_OWN, BF16),
        pltpu.VMEM((D_CHIP, F_OWN), BF16),
        pltpu.VMEM((D_CHIP, F_OWN), BF16),
        pltpu.VMEM((F_OWN, D_CHIP), BF16),
        by_token(F_OWN, F32),
        by_token(F_OWN, BF16),
        z_piece,
        z_piece,
        pltpu.VMEM((4, 2, TOK, F_PART), BF16),
        z_piece,
        z_piece,
        by_token(F_OWN, BF16),
        by_token(F_OWN, F32),
        by_token(F_OWN, F32),
        by_token(F_OWN, BF16),
        by_token(F_OWN, BF16),
        by_token(F_OWN, BF16),
        pltpu.VMEM((2, 2 * TOK, D_CHIP), F32),
        pltpu.VMEM((3, 2, 2 * TOK, D_CHIP), BF16),
        pltpu.VMEM((3, 2, 2 * TOK, D_CHIP), BF16),
        pltpu.VMEM((2, 2 * TOK, D_CHIP), BF16),
        pltpu.VMEM((N_Y, TOK, D_OWN), BF16),
        pltpu.VMEM((F_OWN, D_OWN), BF16),
        pltpu.VMEM((D_OWN, F_OWN), BF16),
        pltpu.VMEM((D_OWN, F_OWN), BF16),
        pltpu.VMEM((F_OWN, D_OWN), BF16),
        pltpu.VMEM((D_OWN, F_OWN), BF16),
        pltpu.VMEM((D_OWN, F_OWN), BF16),
        pltpu.VMEM((F_OWN, D_OWN), F32),
        pltpu.VMEM((D_CHIP, F_OWN), F32),
        pltpu.VMEM((D_CHIP, F_OWN), F32),
        pltpu.VMEM((TOK, D_OWN), BF16),
        pltpu.VMEM((D_OWN, F_OWN), BF16),
        pltpu.VMEM((D_OWN, F_OWN), BF16),
        pltpu.VMEM((F_OWN, D_OWN), BF16),
        pltpu.SemaphoreType.DMA((N_SEMS,)),
        pltpu.SemaphoreType.DMA((N_SEMS,)),
        pltpu.SemaphoreType.DMA((16,)),
        pltpu.SemaphoreType.DMA((8,)),
        pltpu.SemaphoreType.DMA((8,)),
        pltpu.SemaphoreType.DMA((8,)),
    ]
    grads = pl.pallas_call(
        kernel,
        out_shape=outs,
        in_specs=[vmem, vmem] + [hbm] * 5,
        out_specs=(hbm,) * 4,
        scratch_shapes=scratch,
        compiler_params=pltpu.CompilerParams(
            collective_id=0, has_side_effects=True, vmem_limit_bytes=56 * 1024 * 1024
        ),
        cost_estimate=pl.CostEstimate(
            flops=3_700_000_000, bytes_accessed=3_000_000, transcendentals=400_000
        ),
    )(inputs, cotangent, gate_pre, up_pre, gate_weight, up_weight, down_weight)
    return pl.pallas_call(
        copy_kernel,
        out_shape=outs,
        in_specs=[hbm] * 4,
        out_specs=(hbm,) * 4,
        scratch_shapes=[pltpu.VMEM(out.shape, out.dtype) for out in outs]
        + [pltpu.SemaphoreType.DMA((8,))],
    )(*grads)


def solution(mesh):
    placed = (
        P("col", "row"),
        P("col", "row"),
        P("row", "col"),
        P("row", "col"),
        P("row", "col"),
        P("row", "col"),
        P("col", "row"),
    )
    return jax.shard_map(
        on_device,
        mesh=mesh,
        in_specs=placed,
        out_specs=(P("col", "row"), P("row", "col"), P("row", "col"), P("col", "row")),
        check_vma=False,
    )
```

time: 592 us -> 90.5 us (0.15)
  waiting for transfers between devices: 552 us -> 0 us
  Pallas kernels: 0 us -> 89.7 us
  matrix products: 17.6 us -> 0 us
  between operations: 14.2 us -> 0.64 us
    all_gather x5 -> x0, waiting for transfers between devices: 286 us -> none  [the longest x1 86.2 us: on_device(): cotangent_all = lax.all_gather(cotangent, 'col', axis=0, tiled=True)]
    reduce_scatter x2 -> x0, waiting for transfers between devices: 264 us -> none  [the longest x1 203 us: on_device(): lax.psum_scatter((over_columns(gate_all, gate_weight) + over_columns(up_a...]
    pallas_call x0 -> x2, Pallas kernels: none -> 89.7 us  [the longest x1 87.6 us: on_device(): pl.pallas_call(kernel, out_shape=outs, in_specs=[vmem, vmem] + [hbm] * 5,...]
    dot_general x6 -> x0, matrix products: 17.6 us -> none  [the longest x3 9.3 us: over_columns(): lax.dot_general(left, right, (((1,), (1,)), ((), ())), preferred_element_...]
  transfers between devices with their start and end apart: 7 -> 0, of which waited for: 7 -> 0; matrix products, arithmetic and copies ran while one was open for 3% -> 0% of each run, Pallas kernels for 0% -> 0%
where the time goes in v2:
time: 90.5 us; the launch traced here: 90.3 us
  Pallas kernels  89.7 us (99%)
    pallas_call x1, Pallas kernels, on_device(): pl.pallas_call(kernel, out_shape=outs, in_specs=[vmem, vmem] + [hbm] * 5,...  87.6 us
    pallas_call x1, Pallas kernels, on_device(): pl.pallas_call(copy_kernel, out_shape=outs, in_specs=[hbm] * 4, out_specs...  2.09 us

profile of v2, /device:TPU:1, one launch (start us, length us, event | category | flops | bytes accessed | tf_op | source)
XLA Modules:
  0.0 90.3 jit_solution(6237119743200955972)
XLA Ops:
  0.6 87.6 %shard_map.102 = (bf16[48,384]{1,0:T(8,128)(2,1)}, bf16[384,512]{1,0:T(8,128)(2,1)}, bf16[384,512]{1,0:T(8,128)(2,1)}, bf16[512,384]{1,0:T(8,128)(2,1)}) custom-call(bf16[48,384]{1,0:T(8,128)(2,1)} %inp_in.1, bf16[48,384]{1,0:T(8,128)(2,1)} %cot_in.1, bf16[96,512]{1,0:T(8,128)(2,1)} %gate_in.1, bf16[96,512]{1,0:T(8,128)(2,1)} %up_in.1, ...), custom_call_target="tpu_custom_call" | custom-call | flops 3700000000 | bytes 3000000 | tf_op jit(solution)/shard_map/pallas_call | solution.py:517
  88.2 2.1 %shard_map.103 = (bf16[48,384]{1,0:T(8,128)(2,1)}, bf16[384,512]{1,0:T(8,128)(2,1)}, bf16[384,512]{1,0:T(8,128)(2,1)}, bf16[512,384]{1,0:T(8,128)(2,1)}) custom-call(bf16[48,384]{1,0:T(8,128)(2,1)} %get-tuple-element.8.a, bf16[384,512]{1,0:T(8,128)(2,1)} %get-tuple-element.9.b, bf16[384,512]{1,0:T(8,128)(2,1)} %get-tuple-element.10.c, ...), custom_call_target="tpu_custom_call" | custom-call | tf_op jit(solution)/shard_map/pallas_call | solution.py:530

commit v3 on v2

--- a/solution.py
+++ b/solution.py
@@ -16,7 +16,7 @@
 F_OWN = 512
 CHUNK = 192
 F_PART = 128
-N_SEMS = 200
+N_SEMS = 220
 
 
 def nt_dot(left, right):
@@ -36,7 +36,9 @@
     ig_mine, xs_send, xs_got, ys_send, ys_got,
     dg_send, gg_send, ug_send, dg_got, gg_got, ug_got, dg_own, gg_own, ug_own,
     ig_sum, gg_sum, ug_sum, dg_sum,
+    cot_far, inp_far, yf_got, far_sum, far_back,
     send_sems, recv_sems, local_sems, cot_sems, inp_sems, ys_sems,
+    cot_far_sems, inp_far_sems, yf_sems,
 ):
     row = lax.axis_index("row")
     col = lax.axis_index("col")
@@ -73,6 +75,12 @@
         local.append(cp)
         return cp
 
+    lo, hi = pl.ds(0, D_OWN), pl.ds(D_OWN, D_OWN)
+
+    wd_self = move(wd_in, wd.at[:, lo])
+    wg_self = move(wg_in, wg.at[lo])
+    wu_self = move(wu_in, wu.at[lo])
+
     barrier = pltpu.get_barrier_semaphore()
     others = [sib] + [at_y(dy, c) for dy in range(1, N_Y) for c in (0, 1)]
     others += [at_x(dx) for dx in (1, 2, 3)] + [at_z(dz) for dz in (1, 2, 6, 7)]
@@ -80,8 +88,6 @@
         pl.semaphore_signal(barrier, inc=1, device_id=dev, device_id_type=MESH)
     pl.semaphore_wait(barrier, len(others))
 
-    lo, hi = pl.ds(0, D_OWN), pl.ds(D_OWN, D_OWN)
-
     def chunk_of(xx):
         dx = (xx - x + N_X) % N_X
         return dx + (dx // 2) * (5 - 2 * dx)
@@ -91,8 +97,8 @@
     y_sem = (k_y * 2 + h_y) * 2 + side
     late_sends = []
 
-    def over_y(src, buf, sems):
-        dst = buf.at[0, k_y, h_y, :, pl.ds(pl.multiple_of(side * D_OWN, 128), D_OWN)]
+    def over_y(src, buf, r, sems):
+        dst = buf.at[r, k_y, h_y, :, pl.ds(pl.multiple_of(side * D_OWN, 128), D_OWN)]
 
         def copy(k, device):
             return pltpu.make_async_remote_copy(
@@ -100,7 +106,7 @@
                 device_id=device, device_id_type=MESH,
             )
 
-        for dy in (4, 3, 5, 2, 6, 1, 7):
+        for dy in (1, 7, 2, 6, 3, 5, 4):
             cp = copy(len(copies), at_y(dy, c_y))
             cp.start()
             copies.append(cp)
@@ -115,24 +121,32 @@
         def _():
             copy(k, sib).start()
 
-    def over_y_wait(buf, sems):
-        for k in (0, 1):
-            for h in (0, 1):
-                for s, cols in ((0, lo), (1, hi)):
-                    dst = buf.at[0, k, h, :, cols]
-                    pltpu.make_async_copy(dst, dst, sems.at[(k * 2 + h) * 2 + s]).wait()
-
-    def over_x(buf):
-        return [send(buf.at[0], buf.at[r], at_x(dx)) for dx, r in ((2, 3), (1, 2), (3, 1))]
+    def over_y_wait(buf, r, sems, k):
+        for h in (0, 1):
+            for s, cols in ((0, lo), (1, hi)):
+                dst = buf.at[r, k, h, :, cols]
+                pltpu.make_async_copy(dst, dst, sems.at[(k * 2 + h) * 2 + s]).wait()
+
+    k_near = (((y - 2 * core + N_Y) % N_Y + 1) // 4) % 2
+
+    def over_x(buf, k):
+        return {
+            r: send(buf.at[0, k], buf.at[r, k], at_x(dx)) for dx, r in ((1, 2), (3, 1))
+        }
+
+    def over_x_wait(parts, r):
+        for cps in parts:
+            cps[r].wait_recv()
 
     class Ring:
-        def __init__(self, buf, own, long_way):
-            self.buf, self.own = buf, own
+        def __init__(self, buf, own, long_way, h):
+            self.rows = pl.ds(h * TOK, TOK)
+            self.buf, self.own = buf, own.at[self.rows]
             self.hops = {long_way: N_Z // 2, -long_way: N_Z // 2 - 1}
             self.cps = {}
 
         def slot(self, zz):
-            return self.buf.at[chunk_of(zz // 2), zz % 2]
+            return self.buf.at[chunk_of(zz // 2), zz % 2, self.rows]
 
         def start(self, s):
             for way in (+1, -1):
@@ -145,6 +159,10 @@
             for way in (+1, -1):
                 if s <= self.hops[way]:
                     self.cps[way, s].wait_recv()
+
+        def step(self, s):
+            self.wait(s)
+            self.start(s + 1)
 
     def piece(buf, r, dz, rows=pl.ds(0, 2 * TOK)):
         o = (z + dz + N_Z) % N_Z
@@ -252,26 +270,26 @@
     xs_cps = {}
 
     def send_x(r):
-        dx = {1: 1, 2: 3, 3: 2}[r]
+        dx = {1: 1, 2: 3}[r]
         for k in (0, 1):
             xs_cps[r, k] = send(xs_send.at[r - 1, k], xs_got.at[r - 1, k], at_x(dx))
 
-    late_ys = []
-
-    def send_y(k):
+    def sum_x(k):
         total = ig_mine[k]
-        for r in (1, 2, 3):
+        for r in (1, 2):
             xs_cps[r, k].wait_recv()
             total = total + xs_got[r - 1, k].astype(F32)
         ys_send[k] = total.astype(BF16)
+
+    def send_y(src, k, got, sems):
         for h in (0, 1):
             yy = 4 * k + 2 * core + h
             rows = pl.ds(h * TOK, TOK)
 
             def copy(q, cols, on_core, rows=rows, yy=yy):
                 return pltpu.make_async_remote_copy(
-                    src_ref=ys_send.at[k, rows, cols], dst_ref=ys_got.at[y],
-                    send_sem=send_sems.at[q], recv_sem=ys_sems.at[y],
+                    src_ref=src.at[k, rows, cols], dst_ref=got.at[y],
+                    send_sem=send_sems.at[q], recv_sem=sems.at[y],
                     device_id=(z * 2 + on_core, x * N_Y + yy), device_id_type=MESH,
                 )
 
@@ -286,8 +304,16 @@
                 copy(q, lo, core).start()
 
             @pl.when(yy == y)
-            def _(k=k, rows=rows):
-                pltpu.make_async_copy(ys_send.at[k, rows, lo], ys_got.at[y], ys_sems.at[y]).start()
+            def _(rows=rows):
+                pltpu.make_async_copy(src.at[k, rows, lo], got.at[y], sems.at[y]).start()
+
+    def sum_y(got, sems):
+        total = jnp.zeros((TOK, D_OWN), F32)
+        for yy in range(N_Y):
+            dst = got.at[yy]
+            pltpu.make_async_copy(dst, dst, sems.at[yy]).wait()
+            total = total + got[yy].astype(F32)
+        return total
 
     def flat(buf, first, count, width):
         return buf.at[pl.ds(first, count)].reshape(count * CHUNK, width)
@@ -325,120 +351,124 @@
         total[...] = (own[pl.ds(0, total.shape[0]), :] + got[...].astype(F32)).astype(BF16)
         return move(total, out)
 
-    over_y(cot_in, cot, cot_sems)
-    gate_ring = Ring(gate, gate_in, +1)
-    up_ring = Ring(up, up_in, -1)
-    gate_ring.start(1)
-    up_ring.start(1)
-    wd_self = move(wd_in, wd.at[:, lo])
-    wd_cp = send(wd_in, wd.at[:, hi], sib)
-    gate_self = move(gate_in, gate_ring.slot(z))
-    up_self = move(up_in, up_ring.slot(z))
-
-    over_y_wait(cot, cot_sems)
-    cot_cps = over_x(cot)
-    over_y(inp_in, inp, inp_sems)
+    cot_far_cp = send(cot_in, cot_far, at_x(2))
+    over_y(cot_in, cot, 0, cot_sems)
+    rings = [
+        Ring(gate, gate_in, +1, 0), Ring(up, up_in, -1, 0),
+        Ring(gate, gate_in, -1, 1), Ring(up, up_in, +1, 1),
+    ]
+    for ring in rings:
+        ring.start(1)
     wd_self.wait()
+    wd_cp = send(wd.at[:, lo], wd.at[:, hi], sib)
+    gate_self = move(gate_in, gate.at[chunk_of(z // 2), z % 2])
+    up_self = move(up_in, up.at[chunk_of(z // 2), z % 2])
+
+    sums = [SumOverZ(r) for r in range(4)]
+    rings[0].step(1)
+    rings[1].step(1)
+    over_y_wait(cot, 0, cot_sems, k_near)
+    cot_far_cp.wait_recv()
+    over_y(cot_far, cot, 3, cot_far_sems)
+    cot_cps = [over_x(cot, k_near)]
+    rings[2].step(1)
+    rings[3].step(1)
+    rings[0].step(2)
+    over_y_wait(cot, 0, cot_sems, 1 - k_near)
+    cot_cps.append(over_x(cot, 1 - k_near))
+    rings[1].step(2)
+    inp_far_cp = send(inp_in, inp_far, at_x(2))
+    rings[2].step(2)
     wd_cp.wait_recv()
     partial_sums(0)
-    sums = [SumOverZ(r) for r in range(4)]
     sums[0].first()
-    gate_ring.wait(1)
-    gate_ring.start(2)
-    up_ring.wait(1)
-    up_ring.start(2)
-    wg_self = move(wg_in, wg.at[lo])
-    wu_self = move(wu_in, wu.at[lo])
-    wg_cp = send(wg_in, wg.at[hi], sib)
-    wu_cp = send(wu_in, wu.at[hi], sib)
+    rings[3].step(2)
+    wg_self.wait()
+    wg_cp = send(wg.at[lo], wg.at[hi], sib)
+    wu_self.wait()
+    wu_cp = send(wu.at[lo], wu.at[hi], sib)
+    rings[0].step(3)
+    rings[1].step(3)
+    rings[2].step(3)
+    sums[0].second()
+    rings[3].step(3)
+    for r in (2, 1):
+        over_x_wait(cot_cps, r)
+        partial_sums(r)
+        sums[r].first()
+    for k in (0, 1):
+        over_y_wait(cot, 3, cot_far_sems, k)
+    partial_sums(3)
+    sums[3].first()
+    over_y(inp_in, inp, 0, inp_sems)
+    inp_far_cp.wait_recv()
+    over_y(inp_far, inp, 3, inp_far_sems)
+    sums[0].third()
+    sums[2].second()
+    sums[1].second()
+    sums[3].second()
+    inp_cps = []
+    for k in (0, 1):
+        over_y_wait(inp, 0, inp_sems, k)
+        inp_cps.append(over_x(inp, k))
+    sums[0].fourth()
+    sums[2].third()
+    sums[1].third()
+    sums[3].third()
+    for ring in rings:
+        ring.wait(4)
     gate_self.wait()
     up_self.wait()
-
-    sums[0].second()
-    gate_ring.wait(2)
-    gate_ring.start(3)
-    up_ring.wait(2)
-    up_ring.start(3)
-    cot_cps[1].wait_recv()
-    partial_sums(2)
-    sums[2].first()
-    cot_cps[2].wait_recv()
-    partial_sums(1)
-    sums[1].first()
-    sums[0].third()
-    cot_cps[0].wait_recv()
-    partial_sums(3)
-    sums[3].first()
-    over_y_wait(inp, inp_sems)
-    inp_cps = over_x(inp)
-    gate_ring.wait(3)
-    gate_ring.start(4)
-    up_ring.wait(3)
-    up_ring.start(4)
-    sums[2].second()
-    sums[1].second()
-    sums[0].fourth()
-    sums[3].second()
-    sums[2].third()
-    sums[1].third()
-    gate_ring.wait(4)
-    up_ring.wait(4)
     activations(0)
-    sums[3].third()
     activations(2)
-    activations(1)
+    wg_cp.wait_recv()
+    wu_cp.wait_recv()
     sums[2].fourth()
     sums[1].fourth()
+    sums[3].fourth()
+    activations(1)
     activations(3)
-    wg_self.wait()
-    wu_self.wait()
-    wg_cp.wait_recv()
-    wu_cp.wait_recv()
     sums[0].last()
     deltas(0)
     input_part(0)
-    sums[3].fourth()
-    sums[2].last()
-    deltas(2)
-    input_part(2)
-    send_x(2)
-    sums[1].last()
-    deltas(1)
-    input_part(1)
-    send_x(1)
-    dg_cp = down_grad()
+    for r in (2, 1):
+        sums[r].last()
+        deltas(r)
+        input_part(r)
+        send_x(r)
     sums[3].last()
     deltas(3)
     input_part(3)
-    send_x(3)
-    for cp in inp_cps:
-        cp.wait_recv()
-    weight_grad(delta_g, gg_own, 0, 3)
-    weight_grad(delta_g, gg_own, 3, 1, gg_send)
+    for k in (0, 1):
+        send_y(xs_send.at[2], k, yf_got, yf_sems)
+    dg_cp = down_grad()
+    for k in (0, 1):
+        sum_x(k)
+        send_y(ys_send, k, ys_got, ys_sems)
+    for k in (0, 1):
+        over_y_wait(inp, 3, inp_far_sems, k)
+    for r in (1, 2):
+        over_x_wait(inp_cps, r)
+    weight_grad(delta_g, gg_own, 0, 4, gg_send)
     gg_cp = send(gg_send, gg_got, sib)
+    far_sum[...] = sum_y(yf_got, yf_sems).astype(BF16)
+    far_cp = send(far_sum, far_back, at_x(2))
+    weight_grad(delta_u, ug_own, 0, 4, ug_send)
+    ug_cp = send(ug_send, ug_got, sib)
     outs = [finish(dg_own, dg_got, dg_cp, dg_sum, dg_out)]
-    send_y(0)
-    send_y(1)
-    weight_grad(delta_u, ug_own, 0, 3)
-    weight_grad(delta_u, ug_own, 3, 1, ug_send)
-    ug_cp = send(ug_send, ug_got, sib)
     outs.append(finish(gg_own, gg_got, gg_cp, gg_sum, gg_out))
     outs.append(finish(ug_own, ug_got, ug_cp, ug_sum, ug_out))
-
-    total = jnp.zeros((TOK, D_OWN), F32)
-    for yy in range(N_Y):
-        dst = ys_got.at[yy]
-        pltpu.make_async_copy(dst, dst, ys_sems.at[yy]).wait()
-        total = total + ys_got[yy].astype(F32)
-    ig_sum[...] = total.astype(BF16)
-    outs.append(move(ig_sum, ig_out))
-
     for cp in copies:
         cp.wait_send()
     for make, remote in late_sends:
         @pl.when(remote)
         def _(make=make):
             make().wait_send()
+
+    total = sum_y(ys_got, ys_sems)
+    far_cp.wait_recv()
+    ig_sum[...] = (total + far_back[...].astype(F32)).astype(BF16)
+    outs.append(move(ig_sum, ig_out))
     for cp in outs:
         cp.wait()
 
@@ -491,7 +521,7 @@
         by_token(F_OWN, BF16),
         pltpu.VMEM((2, 2 * TOK, D_CHIP), F32),
         pltpu.VMEM((3, 2, 2 * TOK, D_CHIP), BF16),
-        pltpu.VMEM((3, 2, 2 * TOK, D_CHIP), BF16),
+        pltpu.VMEM((2, 2, 2 * TOK, D_CHIP), BF16),
         pltpu.VMEM((2, 2 * TOK, D_CHIP), BF16),
         pltpu.VMEM((N_Y, TOK, D_OWN), BF16),
         pltpu.VMEM((F_OWN, D_OWN), BF16),
@@ -507,17 +537,19 @@
         pltpu.VMEM((D_OWN, F_OWN), BF16),
         pltpu.VMEM((D_OWN, F_OWN), BF16),
         pltpu.VMEM((F_OWN, D_OWN), BF16),
+        pltpu.VMEM((TOK, D_OWN), BF16),
+        pltpu.VMEM((TOK, D_OWN), BF16),
+        pltpu.VMEM((N_Y, TOK, D_OWN), BF16),
+        pltpu.VMEM((TOK, D_OWN), BF16),
+        pltpu.VMEM((TOK, D_OWN), BF16),
         pltpu.SemaphoreType.DMA((N_SEMS,)),
         pltpu.SemaphoreType.DMA((N_SEMS,)),
         pltpu.SemaphoreType.DMA((16,)),
-        pltpu.SemaphoreType.DMA((8,)),
-        pltpu.SemaphoreType.DMA((8,)),
-        pltpu.SemaphoreType.DMA((8,)),
-    ]
+    ] + [pltpu.SemaphoreType.DMA((8,))] * 6
     grads = pl.pallas_call(
         kernel,
         out_shape=outs,
-        in_specs=[vmem, vmem] + [hbm] * 5,
+        in_specs=[vmem] * 4 + [hbm] * 3,
         out_specs=(hbm,) * 4,
         scratch_shapes=scratch,
         compiler_params=pltpu.CompilerParams(

time: 90.5 us -> 79.2 us (0.88); the launches traced: 90.3 us -> 77.6 us
  Pallas kernels: 89.7 us -> 77 us
    pallas_call x1, Pallas kernels: 87.6 us -> 74.9 us  [on_device(): pl.pallas_call(kernel, out_shape=outs, in_specs=[vmem] * 4 + [hbm] * 3, o...]
where the time goes in v3:
time: 79.2 us; the launch traced here: 77.6 us
  Pallas kernels  77 us (97%)
    pallas_call x1, Pallas kernels, on_device(): pl.pallas_call(kernel, out_shape=outs, in_specs=[vmem] * 4 + [hbm] * 3, o...  74.9 us
    pallas_call x1, Pallas kernels, on_device(): pl.pallas_call(copy_kernel, out_shape=outs, in_specs=[hbm] * 4, out_specs...  2.09 us

profile of v3, /device:TPU:1, one launch (start us, length us, event | category | flops | bytes accessed | tf_op | source)
XLA Modules:
  0.0 77.6 jit_solution(14764501154327860662)
XLA Ops:
  0.6 74.9 %shard_map.102 = (bf16[48,384]{1,0:T(8,128)(2,1)}, bf16[384,512]{1,0:T(8,128)(2,1)}, bf16[384,512]{1,0:T(8,128)(2,1)}, bf16[512,384]{1,0:T(8,128)(2,1)}) custom-call(bf16[48,384]{1,0:T(8,128)(2,1)} %inp_in.1, bf16[48,384]{1,0:T(8,128)(2,1)} %cot_in.1, bf16[96,512]{1,0:T(8,128)(2,1)} %gate_in.1, bf16[96,512]{1,0:T(8,128)(2,1)} %up_in.1, ...), custom_call_target="tpu_custom_call" | custom-call | flops 3700000000 | bytes 3000000 | tf_op jit(solution)/shard_map/pallas_call | solution.py:549
  75.6 2.1 %shard_map.103 = (bf16[48,384]{1,0:T(8,128)(2,1)}, bf16[384,512]{1,0:T(8,128)(2,1)}, bf16[384,512]{1,0:T(8,128)(2,1)}, bf16[512,384]{1,0:T(8,128)(2,1)}) custom-call(bf16[48,384]{1,0:T(8,128)(2,1)} %get-tuple-element.8.a, bf16[384,512]{1,0:T(8,128)(2,1)} %get-tuple-element.9.b, bf16[384,512]{1,0:T(8,128)(2,1)} %get-tuple-element.10.c, ...), custom_call_target="tpu_custom_call" | custom-call | tf_op jit(solution)/shard_map/pallas_call | solution.py:562

commit v4 on v3

--- a/solution.py
+++ b/solution.py
@@ -35,7 +35,6 @@
     lin_g, lin_u, hidden, delta_g, delta_u,
     ig_mine, xs_send, xs_got, ys_send, ys_got,
     dg_send, gg_send, ug_send, dg_got, gg_got, ug_got, dg_own, gg_own, ug_own,
-    ig_sum, gg_sum, ug_sum, dg_sum,
     cot_far, inp_far, yf_got, far_sum, far_back,
     send_sems, recv_sems, local_sems, cot_sems, inp_sems, ys_sems,
     cot_far_sems, inp_far_sems, yf_sems,
@@ -346,10 +345,9 @@
         if sent is not None:
             sent[...] = own[hi, :].astype(BF16)
 
-    def finish(own, got, cp, total, out):
+    def finish(own, got, cp, out):
         cp.wait_recv()
-        total[...] = (own[pl.ds(0, total.shape[0]), :] + got[...].astype(F32)).astype(BF16)
-        return move(total, out)
+        out[...] = (own[pl.ds(0, out.shape[0]), :] + got[...].astype(F32)).astype(BF16)
 
     cot_far_cp = send(cot_in, cot_far, at_x(2))
     over_y(cot_in, cot, 0, cot_sems)
@@ -455,9 +453,9 @@
     far_cp = send(far_sum, far_back, at_x(2))
     weight_grad(delta_u, ug_own, 0, 4, ug_send)
     ug_cp = send(ug_send, ug_got, sib)
-    outs = [finish(dg_own, dg_got, dg_cp, dg_sum, dg_out)]
-    outs.append(finish(gg_own, gg_got, gg_cp, gg_sum, gg_out))
-    outs.append(finish(ug_own, ug_got, ug_cp, ug_sum, ug_out))
+    finish(dg_own, dg_got, dg_cp, dg_out)
+    finish(gg_own, gg_got, gg_cp, gg_out)
+    finish(ug_own, ug_got, ug_cp, ug_out)
     for cp in copies:
         cp.wait_send()
     for make, remote in late_sends:
@@ -467,22 +465,15 @@
 
     total = sum_y(ys_got, ys_sems)
     far_cp.wait_recv()
-    ig_sum[...] = (total + far_back[...].astype(F32)).astype(BF16)
-    outs.append(move(ig_sum, ig_out))
-    for cp in outs:
-        cp.wait()
-
-
-def copy_kernel(a, b, c, d, a_out, b_out, c_out, d_out, a_buf, b_buf, c_buf, d_buf, sems):
-    sets = ((a, a_buf, a_out), (b, b_buf, b_out), (c, c_buf, c_out), (d, d_buf, d_out))
-    reads = [pltpu.make_async_copy(src, buf, sems.at[i]) for i, (src, buf, _) in enumerate(sets)]
-    writes = [pltpu.make_async_copy(buf, dst, sems.at[4 + i]) for i, (_, buf, dst) in enumerate(sets)]
-    for cp in reads:
+    ig_out[...] = (total + far_back[...].astype(F32)).astype(BF16)
+
+
+def copy_kernel(a, b, c, d, a_out, b_out, c_out, d_out, sems):
+    pairs = ((a, a_out), (b, b_out), (c, c_out), (d, d_out))
+    cps = [pltpu.make_async_copy(src, dst, sems.at[i]) for i, (src, dst) in enumerate(pairs)]
+    for cp in cps:
         cp.start()
-    for before, cp in zip(reads, writes):
-        before.wait()
-        cp.start()
-    for cp in writes:
+    for cp in cps:
         cp.wait()
 
 
@@ -534,10 +525,6 @@
         pltpu.VMEM((D_CHIP, F_OWN), F32),
         pltpu.VMEM((D_CHIP, F_OWN), F32),
         pltpu.VMEM((TOK, D_OWN), BF16),
-        pltpu.VMEM((D_OWN, F_OWN), BF16),
-        pltpu.VMEM((D_OWN, F_OWN), BF16),
-        pltpu.VMEM((F_OWN, D_OWN), BF16),
-        pltpu.VMEM((TOK, D_OWN), BF16),
         pltpu.VMEM((TOK, D_OWN), BF16),
         pltpu.VMEM((N_Y, TOK, D_OWN), BF16),
         pltpu.VMEM((TOK, D_OWN), BF16),
@@ -548,9 +535,9 @@
     ] + [pltpu.SemaphoreType.DMA((8,))] * 6
     grads = pl.pallas_call(
         kernel,
-        out_shape=outs,
+        out_shape=tuple(pltpu.VMEM(out.shape, out.dtype) for out in outs),
         in_specs=[vmem] * 4 + [hbm] * 3,
-        out_specs=(hbm,) * 4,
+        out_specs=(vmem,) * 4,
         scratch_shapes=scratch,
         compiler_params=pltpu.CompilerParams(
             collective_id=0, has_side_effects=True, vmem_limit_bytes=56 * 1024 * 1024
@@ -562,11 +549,10 @@
     return pl.pallas_call(
         copy_kernel,
         out_shape=outs,
-        in_specs=[hbm] * 4,
+        in_specs=[vmem] * 4,
         out_specs=(hbm,) * 4,
-        scratch_shapes=[pltpu.VMEM(out.shape, out.dtype) for out in outs]
-        + [pltpu.SemaphoreType.DMA((8,))],
-    )(*grads)
+        scratch_shapes=[pltpu.SemaphoreType.DMA((4,))],
+    )(*[pltpu.with_memory_space_constraint(g, pltpu.VMEM) for g in grads])
 
 
 def solution(mesh):

time: 79.2 us -> 77.6 us (0.980)
  Pallas kernels: 77 us -> 75.4 us
    pallas_call x2, Pallas kernels: 77 us -> 75.4 us  [the longest x1 74.3 us: on_device(): pl.pallas_call(kernel, out_shape=tuple((pltpu.VMEM(out.shape, out.dtype)...]
where the time goes in v4:
time: 77.6 us; the launch traced here: 76 us
  Pallas kernels  75.4 us (97%)
    pallas_call x1, Pallas kernels, on_device(): pl.pallas_call(kernel, out_shape=tuple((pltpu.VMEM(out.shape, out.dtype)...  74.3 us

profile of v4, /device:TPU:1, one launch (start us, length us, event | category | flops | bytes accessed | tf_op | source)
XLA Modules:
  0.0 76.0 jit_solution(9423318431885055886)
XLA Ops:
  0.6 74.3 %shard_map.102 = (bf16[48,384]{1,0:T(8,128)(2,1)S(1)}, bf16[384,512]{1,0:T(8,128)(2,1)S(1)}, bf16[384,512]{1,0:T(8,128)(2,1)S(1)}, bf16[512,384]{1,0:T(8,128)(2,1)S(1)}) custom-call(bf16[48,384]{1,0:T(8,128)(2,1)} %inp_in.1, bf16[48,384]{1,0:T(8,128)(2,1)} %cot_in.1, bf16[96,512]{1,0:T(8,128)(2,1)} %gate_in.1, bf16[96,512]{1,0:T(8,128)(2,1)} %up_in.1, ...), custom_call_target="tpu_custom_call" | custom-call | flops 3700000000 | bytes 3000000 | tf_op jit(solution)/shard_map/pallas_call | solution.py:536
  75.0 1.1 %shard_map.103 = (bf16[48,384]{1,0:T(8,128)(2,1)}, bf16[384,512]{1,0:T(8,128)(2,1)}, bf16[384,512]{1,0:T(8,128)(2,1)}, bf16[512,384]{1,0:T(8,128)(2,1)}) custom-call(bf16[48,384]{1,0:T(8,128)(2,1)S(1)} %get-tuple-element.8.a, bf16[384,512]{1,0:T(8,128)(2,1)S(1)} %get-tuple-element.9.b, bf16[384,512]{1,0:T(8,128)(2,1)S(1)} %get-tuple-element.10.c, ...), custom_call_target="tpu_custom_call" | custom-call | tf_op jit(solution)/shard_map/pallas_call | solution.py:549

commit v5 on v4

--- a/solution.py
+++ b/solution.py
@@ -390,14 +390,14 @@
     rings[2].step(3)
     sums[0].second()
     rings[3].step(3)
+    for k in (0, 1):
+        over_y_wait(cot, 3, cot_far_sems, k)
+    partial_sums(3)
+    sums[3].first()
     for r in (2, 1):
         over_x_wait(cot_cps, r)
         partial_sums(r)
         sums[r].first()
-    for k in (0, 1):
-        over_y_wait(cot, 3, cot_far_sems, k)
-    partial_sums(3)
-    sums[3].first()
     over_y(inp_in, inp, 0, inp_sems)
     inp_far_cp.wait_recv()
     over_y(inp_far, inp, 3, inp_far_sems)
@@ -413,17 +413,17 @@
     sums[2].third()
     sums[1].third()
     sums[3].third()
+    wg_cp.wait_recv()
+    wu_cp.wait_recv()
+    sums[2].fourth()
+    sums[1].fourth()
+    sums[3].fourth()
     for ring in rings:
         ring.wait(4)
     gate_self.wait()
     up_self.wait()
     activations(0)
     activations(2)
-    wg_cp.wait_recv()
-    wu_cp.wait_recv()
-    sums[2].fourth()
-    sums[1].fourth()
-    sums[3].fourth()
     activations(1)
     activations(3)
     sums[0].last()

time: 77.6 us -> 78.7 us (1.014)
  the two profiles are of different devices: /device:TPU:1 before, /device:TPU:15 now
where the time goes in v5:
time: 78.7 us; the launch traced here: 78.5 us
  Pallas kernels  77.9 us (99%)
    pallas_call x1, Pallas kernels, on_device(): pl.pallas_call(kernel, out_shape=tuple((pltpu.VMEM(out.shape, out.dtype)...  76.8 us

profile of v5, /device:TPU:15, one launch (start us, length us, event | category | flops | bytes accessed | tf_op | source)
XLA Modules:
  0.0 78.5 jit_solution(477191656797748348)
XLA Ops:
  0.6 76.8 %shard_map.102 = (bf16[48,384]{1,0:T(8,128)(2,1)S(1)}, bf16[384,512]{1,0:T(8,128)(2,1)S(1)}, bf16[384,512]{1,0:T(8,128)(2,1)S(1)}, bf16[512,384]{1,0:T(8,128)(2,1)S(1)}) custom-call(bf16[48,384]{1,0:T(8,128)(2,1)} %inp_in.1, bf16[48,384]{1,0:T(8,128)(2,1)} %cot_in.1, bf16[96,512]{1,0:T(8,128)(2,1)} %gate_in.1, bf16[96,512]{1,0:T(8,128)(2,1)} %up_in.1, ...), custom_call_target="tpu_custom_call" | custom-call | flops 3700000000 | bytes 3000000 | tf_op jit(solution)/shard_map/pallas_call | solution.py:536
  77.5 1.1 %shard_map.103 = (bf16[48,384]{1,0:T(8,128)(2,1)}, bf16[384,512]{1,0:T(8,128)(2,1)}, bf16[384,512]{1,0:T(8,128)(2,1)}, bf16[512,384]{1,0:T(8,128)(2,1)}) custom-call(bf16[48,384]{1,0:T(8,128)(2,1)S(1)} %get-tuple-element.8.a, bf16[384,512]{1,0:T(8,128)(2,1)S(1)} %get-tuple-element.9.b, bf16[384,512]{1,0:T(8,128)(2,1)S(1)} %get-tuple-element.10.c, ...), custom_call_target="tpu_custom_call" | custom-call | tf_op jit(solution)/shard_map/pallas_call | solution.py:549
